TPU v7x, 32 devices: a whole 2x2x4 slice. The times are simulated.
32 devices in a mesh: fsdp: 8 (over z, core), seq: 4 (over y, x).
Axes of the slice: x: 2, y: 2, z: 4, core: 2. Of those that a mesh axis runs over, the one named last changes fastest.
Arguments:
- tokens: bfloat16 [8, 512, 2880], P('fsdp', 'seq'), may hold values from -6 to 6
- queries: bfloat16 [8, 512, 2048], P('fsdp', 'seq'), may hold values from -6 to 6
- kv_weight: bfloat16 [2880, 512], P('fsdp'), may hold values from -0.109375 to 0.109375
- sink_logit_values: float32 [32], replicated, may hold values from 1 to 6
- roll_offsets: int32 [8], P('fsdp'), may hold values from 0 to 511
- out_grad: bfloat16 [8, 512, 2048], P('fsdp', 'seq'), may hold values from -6 to 6
Outputs:
- attn_out: bfloat16 [8, 512, 2048], P('fsdp', 'seq')
- query_grad: bfloat16 [8, 512, 2048], P('fsdp', 'seq')
- token_grad: bfloat16 [8, 512, 2880], P('fsdp', 'seq')
- weight_grad: float32 [4, 2880, 128], P('seq', 'fsdp')
All inputs are finite; a program needn't handle non-finite values.
Results may differ from a plain program's by a relative error of at most 0.012.
Values may be sent and summed in bfloat16 or wider, within the bound.
A program may use at most 64 MiB of HBM per device.

v0:
```python
import functools
import math

import jax
import jax.numpy as jnp
from jax import lax
from jax.experimental import pallas as pl
from jax.experimental.pallas import tpu as pltpu
from jax.sharding import PartitionSpec as P

QUERY_HEADS = 32
KEY_VALUE_HEADS = 4
HEAD_SIZE = 64
WINDOW = 128


rope_base = 150000.0


def from_behind(array, axis, by):
    peers = lax.axis_size(axis)
    pairs = [(i, i + by) for i in range(peers) if 0 <= i + by < peers]
    return lax.ppermute(array, axis, pairs)


def rope_tables(positions):
    half_width = HEAD_SIZE // 2
    frequency = rope_base ** (-jnp.arange(half_width, dtype=jnp.float32) / half_width)
    angle = positions.astype(jnp.float32)[:, None] * frequency[None, :]
    return (jnp.cos(angle), jnp.sin(angle))


def apply_rotary(values, cosine_lookup, sine_lookup, head_count, direction):
    row_count = values.shape[0]
    halves = values.reshape(row_count, head_count, 2, HEAD_SIZE // 2)
    front_half = halves[:, :, 0]
    back_half = halves[:, :, 1]
    cosine_rows = cosine_lookup[:, None, :]
    sine_rows = sine_lookup[:, None, :] * direction
    turned = jnp.stack(
        [
            front_half * cosine_rows - back_half * sine_rows,
            front_half * sine_rows + back_half * cosine_rows,
        ],
        axis=2,
    )
    return turned.reshape(row_count, head_count * HEAD_SIZE)


def attend_group(query_g, key_g, value_g, grad_g, sink_g, allowed):
    score_scale = HEAD_SIZE ** (-0.5)
    scores = (
        jnp.einsum("bgd,kd->gbk", query_g, key_g, preferred_element_type=jnp.float32) * score_scale
    )
    exponent = jnp.where(allowed[None], jnp.exp(scores), 0.0)
    denominator = jnp.exp(sink_g)[:, None] + jnp.sum(exponent, axis=2)
    softmax_w = exponent / denominator[:, :, None]
    softmax_b = softmax_w.astype(jnp.bfloat16)
    attended = jnp.einsum("gbk,kd->bgd", softmax_b, value_g, preferred_element_type=jnp.float32)
    dprob = jnp.einsum("bgd,kd->gbk", grad_g, value_g, preferred_element_type=jnp.float32)
    row_delta = jnp.sum(softmax_w * dprob, axis=2)
    dscore = (softmax_w * (dprob - row_delta[:, :, None]) * score_scale).astype(jnp.bfloat16)
    query_diff = jnp.einsum("gbk,kd->bgd", dscore, key_g, preferred_element_type=jnp.float32)
    key_diff = jnp.einsum("gbk,bgd->kd", dscore, query_g, preferred_element_type=jnp.float32)
    value_diff = jnp.einsum("gbk,bgd->kd", softmax_b, grad_g, preferred_element_type=jnp.float32)
    return (attended.astype(jnp.bfloat16), query_diff, key_diff, value_diff)


def attend_block(query_block, key_block, gradient_block, sink_logit_values, key_first):
    block_row_span = query_block.shape[0]
    key_row_slice = key_block.shape[0]
    group_width = QUERY_HEADS // KEY_VALUE_HEADS
    key_span_width = KEY_VALUE_HEADS * HEAD_SIZE
    rows_idx = jnp.arange(block_row_span, dtype=jnp.int32)[:, None]
    cols_idx = jnp.arange(key_row_slice, dtype=jnp.int32)[None, :]
    allowed = (cols_idx > rows_idx) & (cols_idx <= rows_idx + WINDOW) & (cols_idx + key_first >= 0)
    query_head_rows = query_block.reshape(
        block_row_span, KEY_VALUE_HEADS, group_width, HEAD_SIZE
    ).transpose(1, 0, 2, 3)
    gradient_heads = gradient_block.reshape(
        block_row_span, KEY_VALUE_HEADS, group_width, HEAD_SIZE
    ).transpose(1, 0, 2, 3)
    key_head_rows = (
        key_block[:, :key_span_width]
        .reshape(key_row_slice, KEY_VALUE_HEADS, HEAD_SIZE)
        .transpose(1, 0, 2)
    )
    value_head_rows = (
        key_block[:, key_span_width:]
        .reshape(key_row_slice, KEY_VALUE_HEADS, HEAD_SIZE)
        .transpose(1, 0, 2)
    )
    sink_per_head = sink_logit_values.reshape(KEY_VALUE_HEADS, group_width)

    def per_group(packed):
        return attend_group(packed[0], packed[1], packed[2], packed[3], packed[4], allowed)

    attended, query_diff, key_diff, value_diff = lax.map(
        per_group, (query_head_rows, key_head_rows, value_head_rows, gradient_heads, sink_per_head)
    )
    attended = attended.transpose(1, 0, 2, 3).reshape(block_row_span, QUERY_HEADS * HEAD_SIZE)
    query_diff = query_diff.transpose(1, 0, 2, 3).reshape(block_row_span, QUERY_HEADS * HEAD_SIZE)
    kv_diff = jnp.concatenate(
        [
            key_diff.transpose(1, 0, 2).reshape(key_row_slice, key_span_width),
            value_diff.transpose(1, 0, 2).reshape(key_row_slice, key_span_width),
        ],
        axis=1,
    )
    return (attended, query_diff, kv_diff)


def band_pass(query_rot, keys_all, grad_out, sink_logit_values, row_start):
    row_total = query_rot.shape[0]
    block_row_span = min(row_total, 512)

    def block_step(grad_all, block_index):
        block_begin = block_index * block_row_span
        attended, query_diff, kv_diff = attend_block(
            query_rot, keys_all, grad_out, sink_logit_values, row_start + block_begin - WINDOW
        )
        previous = grad_all
        grad_all = previous + kv_diff
        return (grad_all, (attended, query_diff))

    start_grad = jnp.zeros((row_total + WINDOW, keys_all.shape[1]), jnp.float32)
    grad_all, (attended, query_diff) = lax.scan(
        block_step, start_grad, jnp.arange(row_total // block_row_span, dtype=jnp.int32)
    )
    return (
        attended.reshape(row_total, QUERY_HEADS * HEAD_SIZE),
        query_diff.reshape(row_total, QUERY_HEADS * HEAD_SIZE),
        grad_all,
    )


def local(tokens, queries, kv_weight, sink_logit_values, roll_offsets, out_grad):
    token_rows = tokens[0]
    query_rows = queries[0]
    grad_rows = out_grad[0]
    row_total = token_rows.shape[0]
    key_span_width = KEY_VALUE_HEADS * HEAD_SIZE
    seq_index = lax.axis_index("seq")
    seq_count = lax.axis_size("seq")
    stream_length = row_total * seq_count
    row_start = seq_index * row_total
    whole_weight = lax.all_gather(kv_weight, "fsdp", axis=0, tiled=True)
    projected_rows = jnp.dot(token_rows, whole_weight, preferred_element_type=jnp.float32)
    positions = (
        row_start + jnp.arange(row_total, dtype=jnp.int32) + roll_offsets[0]
    ) % stream_length
    cosine_lookup, sine_lookup = rope_tables(positions)
    key_value_rotated = jnp.concatenate(
        [
            apply_rotary(
                projected_rows[:, :key_span_width], cosine_lookup, sine_lookup, KEY_VALUE_HEADS, 1.0
            ),
            projected_rows[:, key_span_width:],
        ],
        axis=1,
    ).astype(jnp.bfloat16)
    query_rot = apply_rotary(
        query_rows.astype(jnp.float32), cosine_lookup, sine_lookup, QUERY_HEADS, 1.0
    ).astype(jnp.bfloat16)
    edge_rows = from_behind(key_value_rotated, "seq", 1)
    keys_all = jnp.concatenate([edge_rows, key_value_rotated], axis=0)
    attended, query_diff, grad_all = band_pass(
        query_rot, keys_all, grad_rows, sink_logit_values, row_start
    )
    incoming = from_behind(grad_all[:WINDOW].astype(jnp.bfloat16), "seq", -1).astype(jnp.float32)
    local_gradient = grad_all[WINDOW:]
    local_gradient = jnp.concatenate(
        [local_gradient[: row_total - WINDOW], local_gradient + incoming], axis=0
    )
    query_back = apply_rotary(query_diff, cosine_lookup, sine_lookup, QUERY_HEADS, -1.0).astype(
        jnp.bfloat16
    )
    key_value_backward = jnp.concatenate(
        [
            apply_rotary(
                local_gradient[:, :key_span_width],
                cosine_lookup,
                sine_lookup,
                KEY_VALUE_HEADS,
                -1.0,
            ),
            local_gradient[:, key_span_width:],
        ],
        axis=1,
    ).astype(jnp.bfloat16)
    token_back = lax.dot_general(
        key_value_backward,
        whole_weight,
        (((1,), (1,)), ((), ())),
        preferred_element_type=jnp.float32,
    ).astype(jnp.bfloat16)
    feature_block = lax.all_to_all(token_rows, "seq", split_axis=1, concat_axis=0, tiled=True)
    block_term = lax.dot_general(
        feature_block,
        lax.all_gather(key_value_backward, "seq", axis=0, tiled=True),
        (((0,), (0,)), ((), ())),
        preferred_element_type=jnp.float32,
    )
    flat_block = block_term.reshape(-1, 128)
    weight_share = lax.psum_scatter(flat_block, "fsdp", scatter_dimension=0, tiled=True)
    return (attended[None], query_back[None], token_back[None], weight_share[None])


def nt(a, b):
    return lax.dot_general(a, b, (((1,), (1,)), ((), ())), preferred_element_type=jnp.float32)


def tn(a, b):
    return lax.dot_general(a, b, (((0,), (0,)), ((), ())), preferred_element_type=jnp.float32)


def nn(a, b):
    return lax.dot_general(a, b, (((1,), (0,)), ((), ())), preferred_element_type=jnp.float32)


def turn(x, cosine, sine, back):
    width = x.shape[1]
    lane = lax.broadcasted_iota(jnp.int32, x.shape, 1)
    swapped = jnp.where(
        lane % HEAD_SIZE < HEAD_SIZE // 2,
        pltpu.roll(x, width - HEAD_SIZE // 2, 1),
        pltpu.roll(x, HEAD_SIZE // 2, 1),
    )
    times = width // cosine.shape[1]
    cosine = jnp.concatenate([cosine] * times, axis=1)
    sine = jnp.concatenate([sine] * times, axis=1)
    if back:
        return x * cosine - swapped * sine
    return x * cosine + swapped * sine


def fused_kernel(
    nz, ns, share, pad,
    tok_hbm, q_hbm, w, sinks, rolls, og_hbm,
    attn_v, qgrad_v, tgrad_v, wgrad,
    wall, tok, q, og, tokf, tokpad, tokblk, qs, gs, kvbuf, prob_t, dscore_t,
    own_g, hg_out, hg_in, dkv_all, core_out, core_in, mine, zsum, z_out, z_in, total, esink,
    ins, rs_l, rr_l, rs_r, rr_r, qsn, qrn, ps, pr, ts, tr, hs, hr, gsn, grn, dsn, drn, cs, cr, rs, rr,
):
    nf = 2 * nz
    rows = q.shape[0]
    krows = w.shape[0]
    groups = KEY_VALUE_HEADS
    per = QUERY_HEADS // KEY_VALUE_HEADS
    span = per * HEAD_SIZE
    half = nz * pad
    f = lax.axis_index("fsdp")
    s = lax.axis_index("seq")
    z = f // 2
    c = f % 2
    partner = (f + 1 - 2 * c, s)

    def zpeer(d):
        return lax.rem(z + d, nz) * 2 + c

    def speer(d):
        return lax.rem(s + d, ns)

    def remote(src, dst, a, b, dev):
        return pltpu.make_async_remote_copy(
            src_ref=src, dst_ref=dst, send_sem=a, recv_sem=b,
            device_id=dev, device_id_type=pl.DeviceIdType.MESH,
        )

    def lanes_of(i, size):
        return pl.ds(pl.multiple_of(i * size, 128), size)

    cols = lanes_of(s, 128)
    loads = [
        pltpu.make_async_copy(tok_hbm, tok, ins.at[0]),
        pltpu.make_async_copy(q_hbm, q, ins.at[1]),
        pltpu.make_async_copy(og_hbm, og, ins.at[2]),
    ]
    for j in range(ns):
        own = w.at[:, j * 128 : (j + 1) * 128]
        loads.append(pltpu.make_async_copy(own, wall.at[j, f], ins.at[3 + j]))
    for cp in loads:
        cp.start()

    barrier = pltpu.get_barrier_semaphore()
    for d in range(1, nz):
        pl.semaphore_signal(barrier, inc=1, device_id=(zpeer(d), s), device_id_type=pl.DeviceIdType.MESH)
    for d in range(1, ns):
        pl.semaphore_signal(barrier, inc=1, device_id=(f, speer(d)), device_id_type=pl.DeviceIdType.MESH)
    pl.semaphore_signal(barrier, inc=1, device_id=partner, device_id_type=pl.DeviceIdType.MESH)
    pl.semaphore_wait(barrier, nz + ns - 1)

    sent = []

    def send(*args):
        cp = remote(*args)
        cp.start()
        sent.append(cp)

    def chain(k, right):
        at = z + k if right else z - k
        there = at < nz if right else at >= 0
        onward = z >= 1 if right else z + 1 < nz
        onto = ((z - 1 if right else z + 1) * 2 + c, s)
        return at * 2 + c, there, onward, onto

    def link(k, right):
        block, _, _, onto = chain(k, right)
        a, b = (rs_r, rr_r) if right else (rs_l, rr_l)
        piece = wall.at[s, block]
        source = w.at[:, cols] if k == 0 else piece
        return remote(source, piece, a.at[k], b.at[k], onto)

    def arrived(k, right):
        block, _, _, onto = chain(k, right)
        b = rr_r if right else rr_l
        piece = wall.at[s, block]
        return remote(piece, piece, rs_l.at[0], b.at[k - 1], onto)

    def over_seq(block, e):
        piece = wall.at[s, block]
        return remote(piece, piece, qsn.at[block // 2, e - 1], qrn.at[block // 2, e - 1], (f, speer(e)))

    def over_core(block):
        piece = wall.at[:, block]
        return remote(piece, piece, ps.at[block // 2], pr.at[block // 2], partner)

    ways = [(k, right) for k in range(1, nz) for right in (False, True)]

    for right in (False, True):

        @pl.when(chain(0, right)[2])
        def _(right=right):
            link(0, right).start()

    for cp in loads[3:]:
        cp.wait()
    over_core(f).start()

    loads[0].wait()
    for i in range(nf):
        tokf[i, :, :krows] = tok[i * krows : (i + 1) * krows, :].T

    for k, right in ways:
        block, there, onward, _ = chain(k, right)

        @pl.when(there)
        def _(k=k, right=right, block=block):
            arrived(k, right).wait_recv()
            for e in range(1, ns):
                over_seq(block, e).start()

        @pl.when(there & onward)
        def _(k=k, right=right):
            link(k, right).start()

    lane = lax.broadcasted_iota(jnp.int32, (rows, 128), 1)
    turn_lane = (lane % (HEAD_SIZE // 2)).astype(jnp.float32) / (HEAD_SIZE // 2)
    frequency = jnp.exp(turn_lane * (-math.log(rope_base)))
    position = lax.rem(
        s * rows + rolls[0] + lax.broadcasted_iota(jnp.int32, (rows, 128), 0), rows * ns
    )
    angle = position.astype(jnp.float32) * frequency
    cosine = jnp.cos(angle)
    sine = jnp.sin(angle)
    sine = jnp.where(lane % HEAD_SIZE < HEAD_SIZE // 2, -sine, sine)
    for p in range(QUERY_HEADS // 2):
        pair = [jnp.full((1, rows), sinks[2 * p + i], jnp.float32) for i in range(2)]
        esink[p] = jnp.exp(jnp.concatenate(pair, axis=1))

    tokpad[...] = jnp.zeros_like(tokpad)
    for t in range(ns):
        for j in range(2):
            for i in range(nz):
                start = (t * nf + 2 * i + j) * share
                to = (j * nz + i) * pad
                tokpad[t, to : to + share, :] = tok[start : start + share, :]
    tokblk[s] = tokpad[s]

    loads[1].wait()
    loads[2].wait()

    @pl.loop(0, groups)
    def _(g):
        here = lanes_of(g, span)
        x = turn(q[:, here].astype(jnp.float32), cosine, sine, False).astype(jnp.bfloat16)
        x = x * jnp.asarray(HEAD_SIZE ** (-0.5), jnp.bfloat16)
        o = og[:, here]
        for h in range(per):
            qs[g, h * rows : (h + 1) * rows, :] = x[:, h * HEAD_SIZE : (h + 1) * HEAD_SIZE]
            gs[g, h * rows : (h + 1) * rows, :] = o[:, h * HEAD_SIZE : (h + 1) * HEAD_SIZE]

    def whole(block):
        return jnp.concatenate([wall[j, block] for j in range(ns)], axis=1)

    def part(block):
        return nn(tokf[block][:, :krows], whole(block))

    total[...] = part(f)
    other = f + 1 - 2 * c
    over_core(other).wait_recv()
    total[...] += part(other)
    for k, right in ways:
        block, there, _, _ = chain(k, right)

        @pl.when(there)
        def _(block=block):
            for e in range(1, ns):
                piece = wall.at[lax.rem(s + ns - e, ns), block]
                remote(
                    piece, piece, qsn.at[block // 2, e - 1], qrn.at[block // 2, e - 1], (f, speer(e))
                ).wait_recv()
            over_core(block).start()
            total[...] += part(block)

    for k, right in ways:
        block, there, _, _ = chain(k, right)

        @pl.when(there)
        def _(block=block):
            over_core(block + 1 - 2 * c).wait_recv()
            total[...] += part(block + 1 - 2 * c)

    key_width = groups * HEAD_SIZE
    keys = turn(total[:, :key_width], cosine, sine, False).astype(jnp.bfloat16)
    values = total[:, key_width:].astype(jnp.bfloat16)
    for g in range(groups):
        lo, hi = g * HEAD_SIZE, (g + 1) * HEAD_SIZE
        kvbuf[g, WINDOW:, :] = jnp.concatenate([keys[:, lo:hi], values[:, lo:hi]], axis=1)
    halo = remote(
        kvbuf.at[:, pl.ds(WINDOW, WINDOW), :], kvbuf.at[:, pl.ds(0, WINDOW), :], hs, hr, (f, speer(1))
    )
    halo.start()
    halo.wait()
    for e in range(1, ns):
        send(tokpad.at[speer(e)], tokblk.at[s], ts.at[e - 1], tr.at[e - 1], (f, speer(e)))
    before = speer(ns - 1)
    mine_rows = pl.ds(pl.multiple_of(s * rows, 128), rows)

    def hg_copy(g):
        return remote(hg_out.at[g], hg_in.at[g], gsn.at[g], grn.at[g], (f, before))

    def attention(g):
        kv = kvbuf[g]
        key, value = kv[:, :HEAD_SIZE], kv[:, HEAD_SIZE:]
        kv_t = kv.T
        key_t, value_t = kv_t[:HEAD_SIZE], kv_t[HEAD_SIZE:]
        slot = lax.broadcasted_iota(jnp.int32, (rows, 2 * rows), 0)
        at = lax.broadcasted_iota(jnp.int32, (rows, 2 * rows), 1) & (rows - 1)
        is_own = slot <= at
        valid = slot <= at + s * rows

        def chosen(x):
            return jnp.where(is_own, x[WINDOW:], x[:WINDOW])

        def spread(x):
            borrowed = jnp.where(is_own, 0.0, x)
            return jnp.concatenate([borrowed, jnp.where(is_own, x, 0.0)], axis=0).astype(jnp.bfloat16)

        for p in range(per // 2):
            two = slice(p * 2 * rows, (p + 1) * 2 * rows)
            query, grad = qs[g, two, :], gs[g, two, :]
            expo = jnp.where(valid, jnp.exp(chosen(nt(key, query))), 0.0)
            denominator = esink[g * (per // 2) + p] + jnp.sum(expo, axis=0, keepdims=True)
            probs = expo * (1.0 / denominator)
            dprob = chosen(nt(value, grad))
            delta = jnp.sum(probs * dprob, axis=0, keepdims=True)
            probs_b = spread(probs)
            dscore = spread(probs * (dprob - delta))
            prob_t[:, two] = probs_b
            dscore_t[:, two] = dscore
            out = nn(value_t, probs_b)
            dq = nn(key_t, dscore) * (HEAD_SIZE ** (-0.5))
            out = jnp.concatenate([out[:, :rows], out[:, rows:]], axis=0).T
            dq = jnp.concatenate([dq[:, :rows], dq[:, rows:]], axis=0).T
            here = pl.ds(pl.multiple_of(g * span + p * 128, 128), 128)
            attn_v[:, here] = out.astype(jnp.bfloat16)
            qgrad_v[:, here] = turn(dq, cosine, sine, True).astype(jnp.bfloat16)
        dkv = jnp.concatenate([nn(dscore_t[...], qs[g]), nn(prob_t[...], gs[g])], axis=1)
        hg_out[g] = dkv[:WINDOW].astype(jnp.bfloat16)
        own_g[g] = dkv[WINDOW:]
        hg_copy(g).start()

    def dkv_copy(g, e):
        piece = dkv_all.at[g, mine_rows, :]
        return remote(piece, piece, dsn.at[g, e - 1], drn.at[g, e - 1], (f, speer(e)))

    def finish(g):
        hg_copy(g).wait_recv()
        both = own_g[g] + hg_in[g].astype(jnp.float32)
        lane = lax.broadcasted_iota(jnp.int32, both.shape, 1)
        dkv = jnp.where(lane < HEAD_SIZE, turn(both, cosine, sine, True), both)
        dkv_all[g, mine_rows, :] = dkv.astype(jnp.bfloat16)
        for e in range(1, ns):
            dkv_copy(g, e).start()

    def core_copy(g):
        return remote(core_out.at[g], core_in.at[g], cs.at[g], cr.at[g], partner)

    def features(core):
        there = pl.ds(pl.multiple_of(core * half, 128), half)
        return jnp.concatenate([tokblk[t, there, :] for t in range(ns)], axis=1)

    def weight_part(g):
        for e in range(1, ns):
            src = lax.rem(s + ns - e, ns)
            piece = dkv_all.at[g, pl.ds(pl.multiple_of(src * rows, 128), rows), :]
            remote(piece, piece, dsn.at[g, e - 1], drn.at[g, e - 1], (f, src)).wait_recv()
        dkv = dkv_all[g]
        core_out[g] = nn(features(1 - c), dkv).astype(jnp.bfloat16)
        core_copy(g).start()
        mine[g] = nn(features(c), dkv)

    def z_copy(g, d):
        return remote(z_out.at[g, d - 1], z_in.at[g, d - 1], rs.at[g, d - 1], rr.at[g, d - 1], (zpeer(d), s))

    def z_part(g):
        core_copy(g).wait_recv()
        zsum[g] = (mine[g] + core_in[g].astype(jnp.float32)).reshape(nz, pad, 128)
        for d in range(1, nz):
            z_out[g, d - 1] = zsum[g, lax.rem(z + d, nz)].astype(jnp.bfloat16)
            z_copy(g, d).start()

    def token_blocks():
        for e in range(1, ns):
            src = lax.rem(s + ns - e, ns)
            remote(tokpad.at[src], tokblk.at[src], ts.at[e - 1], tr.at[e - 1], (f, src)).wait_recv()

    @pl.loop(0, groups)
    def _(g):
        attention(g)

        @pl.when(g >= 1)
        def _():
            finish(g - 1)

        @pl.when(g == 2)
        def _():
            token_blocks()

        @pl.when(g >= 2)
        def _():
            weight_part(g - 2)

        @pl.when(g >= 3)
        def _():
            z_part(g - 3)

    finish(groups - 1)
    weight_part(groups - 2)
    z_part(groups - 3)
    pieces = [dkv_all[g, mine_rows, :] for g in range(groups)]
    dkv = jnp.concatenate([b[:, :HEAD_SIZE] for b in pieces] + [b[:, HEAD_SIZE:] for b in pieces], axis=1)
    for i in range(nf):
        tgrad_v[i * krows : (i + 1) * krows, :] = nt(whole(i), dkv).astype(jnp.bfloat16)
    weight_part(groups - 1)
    z_part(groups - 2)
    z_part(groups - 1)

    sums = []
    for g in range(groups):
        acc = zsum[g, z]
        for d in range(1, nz):
            z_copy(g, d).wait_recv()
            acc = acc + z_in[g, d - 1].astype(jnp.float32)
        sums.append(acc[:share])
    order = []
    for lo in (0, HEAD_SIZE):
        for g in range(0, groups, 2):
            order.append(jnp.concatenate([sums[g][:, lo : lo + HEAD_SIZE], sums[g + 1][:, lo : lo + HEAD_SIZE]], axis=1))
    for j in range(groups):
        wgrad[pl.ds(j, share, stride=groups), :] = order[j]

    for cp in sent:
        cp.wait_send()
    for g in range(groups):
        hg_copy(g).wait_send()
        core_copy(g).wait_send()
        for e in range(1, ns):
            dkv_copy(g, e).wait_send()
        for d in range(1, nz):
            z_copy(g, d).wait_send()
    for k in range(nz):
        for right in (False, True):
            _, there, onward, _ = chain(k, right)

            @pl.when(there & onward)
            def _(k=k, right=right):
                link(k, right).wait_send()

            if k > 0:

                @pl.when(there)
                def _(k=k, right=right):
                    block = chain(k, right)[0]
                    for e in range(1, ns):
                        over_seq(block, e).wait_send()
                    over_core(block).wait_send()

    over_core(f).wait_send()


def write_out(*refs):
    done = refs[8]
    copies = [pltpu.make_async_copy(refs[i], refs[4 + i], done.at[i]) for i in range(4)]
    for cp in copies:
        cp.start()
    for cp in copies:
        cp.wait()


KW_COLUMNS = 2 * KEY_VALUE_HEADS * HEAD_SIZE


def fused(tokens, queries, kv_weight, sink_logit_values, roll_offsets, out_grad):
    nf = lax.axis_size("fsdp")
    ns = lax.axis_size("seq")
    nz = nf // 2
    rows, width = tokens.shape[1:]
    krows = kv_weight.shape[0]
    share = width // (nf * ns)
    pad = -(-share // 16) * 16
    half = nz * pad
    query_width = QUERY_HEADS * HEAD_SIZE
    groups = KEY_VALUE_HEADS
    per = QUERY_HEADS // groups
    bf, f32 = jnp.bfloat16, jnp.float32
    sem = pltpu.SemaphoreType.DMA
    vm = pltpu.VMEM
    shape = jax.ShapeDtypeStruct
    anywhere = pl.BlockSpec(memory_space=pl.ANY)
    inside = pl.BlockSpec(memory_space=pltpu.VMEM)
    scalars = pl.BlockSpec(memory_space=pltpu.SMEM)
    results = pl.pallas_call(
        functools.partial(fused_kernel, nz, ns, share, pad),
        out_shape=(
            shape((rows, query_width), bf),
            shape((rows, query_width), bf),
            shape((width, rows), bf),
            shape((share * groups, 128), f32),
        ),
        in_specs=[anywhere, anywhere, anywhere, scalars, scalars, anywhere],
        out_specs=[inside] * 4,
        scratch_shapes=[
            vm((ns, nf, krows, 128), bf),
            vm((width, rows), bf),
            vm((rows, query_width), bf),
            vm((rows, query_width), bf),
            vm((nf, rows, -(-krows // 128) * 128), bf),
            vm((ns, nf * pad, rows), bf),
            vm((ns, nf * pad, rows), bf),
            vm((groups, per * rows, HEAD_SIZE), bf),
            vm((groups, per * rows, HEAD_SIZE), bf),
            vm((groups, rows + WINDOW, 2 * HEAD_SIZE), bf),
            vm((rows + WINDOW, per * rows), bf),
            vm((rows + WINDOW, per * rows), bf),
            vm((groups, rows, 2 * HEAD_SIZE), f32),
            vm((groups, WINDOW, 2 * HEAD_SIZE), bf),
            vm((groups, WINDOW, 2 * HEAD_SIZE), bf),
            vm((groups, ns * rows, 2 * HEAD_SIZE), bf),
            vm((groups, half, 128), bf),
            vm((groups, half, 128), bf),
            vm((groups, half, 128), f32),
            vm((groups, nz, pad, 128), f32),
            vm((groups, nz - 1, pad, 128), bf),
            vm((groups, nz - 1, pad, 128), bf),
            vm((rows, KW_COLUMNS), f32),
            vm((QUERY_HEADS // 2, 1, 2 * rows), f32),
            sem((3 + ns,)),
            sem((nz,)), sem((nz,)), sem((nz,)), sem((nz,)),
            sem((nz, ns - 1)), sem((nz, ns - 1)),
            sem((nz,)), sem((nz,)),
            sem((ns - 1,)), sem((ns - 1,)),
            sem, sem,
            sem((groups,)), sem((groups,)),
            sem((groups, ns - 1)), sem((groups, ns - 1)),
            sem((groups,)), sem((groups,)),
            sem((groups, nz - 1)), sem((groups, nz - 1)),
        ],
        compiler_params=pltpu.CompilerParams(
            collective_id=0, has_side_effects=True, vmem_limit_bytes=56 * 1024 * 1024
        ),
    )(tokens[0].T, queries[0], kv_weight, sink_logit_values, roll_offsets, out_grad[0])
    attn, qgrad, tgrad, wgrad = pl.pallas_call(
        write_out,
        out_shape=tuple(shape(x.shape, x.dtype) for x in results),
        in_specs=[inside] * 4,
        out_specs=[anywhere] * 4,
        scratch_shapes=[sem((4,))],
    )(*results)
    return (attn[None], qgrad[None], tgrad.T[None], wgrad[None])


def fits_fused(mesh):
    nf, ns = mesh.shape["fsdp"], mesh.shape["seq"]
    return nf == 8 and KW_COLUMNS == 128 * ns


def solution(mesh):
    placed = (
        P("fsdp", "seq", None),
        P("fsdp", "seq", None),
        P("fsdp", None),
        P(),
        P("fsdp"),
        P("fsdp", "seq", None),
    )
    return jax.shard_map(
        fused if fits_fused(mesh) else local,
        mesh=mesh,
        in_specs=placed,
        out_specs=(
            P("fsdp", "seq", None),
            P("fsdp", "seq", None),
            P("fsdp", "seq", None),
            P("seq", "fsdp", None),
        ),
        check_vma=False,
    )
```

profile of v0, /device:TPU:0, one launch (start us, length us, event | category | flops | bytes accessed | tf_op | source)
XLA Modules:
  0.0 67.8 jit_solution(15122088725758511310)
XLA Ops:
  1.3 63.7 %shard_map.93 = (bf16[128,2048]{1,0:T(8,128)(2,1)}, bf16[128,2048]{1,0:T(8,128)(2,1)}, bf16[2880,128]{1,0:T(8,128)(2,1)}, f32[360,128]{1,0:T(8,128)}) custom-call(bf16[2880,128]{1,0:T(8,128)(2,1)} %bitcast.11, bf16[128,2048]{1,0:T(8,128)(2,1)} %bitcast.12, bf16[360,512]{1,0:T(8,128)(2,1)} %w.1, f32[32]{0:T(128)} %sinks.1, s32[1]{0:T(128)S(6)} %copy.10.rolls, ...), custom_call_target="tpu_custom_call" | custom-call | tf_op jit(solution)/shard_map/pallas_call | solution.py:634
  65.0 2.8 %shard_map.94 = (bf16[128,2048]{1,0:T(8,128)(2,1)}, bf16[128,2048]{1,0:T(8,128)(2,1)}, bf16[2880,128]{1,0:T(8,128)(2,1)}, f32[360,128]{1,0:T(8,128)}) custom-call(bf16[128,2048]{1,0:T(8,128)(2,1)} %get-tuple-element.12.refs_0_, bf16[128,2048]{1,0:T(8,128)(2,1)} %get-tuple-element.13.refs_1_, bf16[2880,128]{1,0:T(8,128)(2,1)} %get-tuple-element.14.refs_2_, ...), custom_call_target="tpu_custom_call" | custom-call | tf_op jit(solution)/shard_map/pallas_call | solution.py:684
where the time goes:
time: 67.9 us; the launch traced here: 67.8 us
  Pallas kernels  66.5 us (98%)
  between operations  1.29 us (2%)
    pallas_call x1, Pallas kernels, fused(): pl.pallas_call(functools.partial(fused_kernel, nz, ns, share, pad), out_s...  63.7 us
    pallas_call x1, Pallas kernels, fused(): pl.pallas_call(write_out, out_shape=tuple((shape(x.shape, x.dtype) for x...  2.76 us

commit v1 on v0

--- a/solution.py
+++ b/solution.py
@@ -288,72 +288,6 @@
     for d in range(1, ns):
         pl.semaphore_signal(barrier, inc=1, device_id=(f, speer(d)), device_id_type=pl.DeviceIdType.MESH)
     pl.semaphore_signal(barrier, inc=1, device_id=partner, device_id_type=pl.DeviceIdType.MESH)
-    pl.semaphore_wait(barrier, nz + ns - 1)
-
-    sent = []
-
-    def send(*args):
-        cp = remote(*args)
-        cp.start()
-        sent.append(cp)
-
-    def chain(k, right):
-        at = z + k if right else z - k
-        there = at < nz if right else at >= 0
-        onward = z >= 1 if right else z + 1 < nz
-        onto = ((z - 1 if right else z + 1) * 2 + c, s)
-        return at * 2 + c, there, onward, onto
-
-    def link(k, right):
-        block, _, _, onto = chain(k, right)
-        a, b = (rs_r, rr_r) if right else (rs_l, rr_l)
-        piece = wall.at[s, block]
-        source = w.at[:, cols] if k == 0 else piece
-        return remote(source, piece, a.at[k], b.at[k], onto)
-
-    def arrived(k, right):
-        block, _, _, onto = chain(k, right)
-        b = rr_r if right else rr_l
-        piece = wall.at[s, block]
-        return remote(piece, piece, rs_l.at[0], b.at[k - 1], onto)
-
-    def over_seq(block, e):
-        piece = wall.at[s, block]
-        return remote(piece, piece, qsn.at[block // 2, e - 1], qrn.at[block // 2, e - 1], (f, speer(e)))
-
-    def over_core(block):
-        piece = wall.at[:, block]
-        return remote(piece, piece, ps.at[block // 2], pr.at[block // 2], partner)
-
-    ways = [(k, right) for k in range(1, nz) for right in (False, True)]
-
-    for right in (False, True):
-
-        @pl.when(chain(0, right)[2])
-        def _(right=right):
-            link(0, right).start()
-
-    for cp in loads[3:]:
-        cp.wait()
-    over_core(f).start()
-
-    loads[0].wait()
-    for i in range(nf):
-        tokf[i, :, :krows] = tok[i * krows : (i + 1) * krows, :].T
-
-    for k, right in ways:
-        block, there, onward, _ = chain(k, right)
-
-        @pl.when(there)
-        def _(k=k, right=right, block=block):
-            arrived(k, right).wait_recv()
-            for e in range(1, ns):
-                over_seq(block, e).start()
-
-        @pl.when(there & onward)
-        def _(k=k, right=right):
-            link(k, right).start()
-
     lane = lax.broadcasted_iota(jnp.int32, (rows, 128), 1)
     turn_lane = (lane % (HEAD_SIZE // 2)).astype(jnp.float32) / (HEAD_SIZE // 2)
     frequency = jnp.exp(turn_lane * (-math.log(rope_base)))
@@ -367,6 +301,82 @@
     for p in range(QUERY_HEADS // 2):
         pair = [jnp.full((1, rows), sinks[2 * p + i], jnp.float32) for i in range(2)]
         esink[p] = jnp.exp(jnp.concatenate(pair, axis=1))
+
+    pl.semaphore_wait(barrier, nz + ns - 1)
+
+    sent = []
+
+    def send(*args):
+        cp = remote(*args)
+        cp.start()
+        sent.append(cp)
+
+    def chain(k, right):
+        at = z + k if right else z - k
+        there = at < nz if right else at >= 0
+        onward = z >= 1 if right else z + 1 < nz
+        onto = ((z - 1 if right else z + 1) * 2 + c, s)
+        return at * 2 + c, there, onward, onto
+
+    def link(k, right):
+        block, _, _, onto = chain(k, right)
+        a, b = (rs_r, rr_r) if right else (rs_l, rr_l)
+        piece = wall.at[s, block]
+        source = w.at[:, cols] if k == 0 else piece
+        return remote(source, piece, a.at[k], b.at[k], onto)
+
+    def arrived(k, right):
+        block, _, _, onto = chain(k, right)
+        b = rr_r if right else rr_l
+        piece = wall.at[s, block]
+        return remote(piece, piece, rs_l.at[0], b.at[k - 1], onto)
+
+    across = s + 1 - 2 * (s % 2)
+    along = s + 2 - 4 * (s // 2)
+    corner = ns - 1 - s
+
+    def over_seq(owner, block, e, peer):
+        piece = wall.at[owner, block]
+        return remote(piece, piece, qsn.at[block // 2, e], qrn.at[block // 2, e], (f, peer))
+
+    def relay(block):
+        way = (block // 2 + c) % 2
+        owner = across + way * (along - across)
+        peer = along + way * (across - along)
+        return over_seq(owner, block, 2, peer)
+
+    def over_core(block):
+        piece = wall.at[:, block]
+        return remote(piece, piece, ps.at[block // 2], pr.at[block // 2], partner)
+
+    ways = [(k, right) for k in range(1, nz) for right in (False, True)]
+
+    for right in (False, True):
+
+        @pl.when(chain(0, right)[2])
+        def _(right=right):
+            link(0, right).start()
+
+    for cp in loads[3:]:
+        cp.wait()
+    over_core(f).start()
+
+    loads[0].wait()
+    for i in range(nf):
+        tokf[i, :, :krows] = tok[i * krows : (i + 1) * krows, :].T
+
+    for k, right in ways:
+        block, there, onward, _ = chain(k, right)
+
+        @pl.when(there)
+        def _(k=k, right=right, block=block):
+            arrived(k, right).wait_recv()
+            over_seq(s, block, 0, across).start()
+            over_seq(s, block, 1, along).start()
+
+        @pl.when(there & onward)
+        def _(k=k, right=right):
+            link(k, right).start()
 
     tokpad[...] = jnp.zeros_like(tokpad)
     for t in range(ns):
@@ -380,8 +390,9 @@
     loads[1].wait()
     loads[2].wait()
 
-    @pl.loop(0, groups)
-    def _(g):
+    def stack_heads(g):
+        if g >= groups:
+            return
         here = lanes_of(g, span)
         x = turn(q[:, here].astype(jnp.float32), cosine, sine, False).astype(jnp.bfloat16)
         x = x * jnp.asarray(HEAD_SIZE ** (-0.5), jnp.bfloat16)
@@ -396,23 +407,35 @@
     def part(block):
         return nn(tokf[block][:, :krows], whole(block))
 
-    total[...] = part(f)
-    other = f + 1 - 2 * c
-    over_core(other).wait_recv()
-    total[...] += part(other)
-    for k, right in ways:
+    def pass_on(k, right):
         block, there, _, _ = chain(k, right)
 
         @pl.when(there)
-        def _(block=block):
-            for e in range(1, ns):
-                piece = wall.at[lax.rem(s + ns - e, ns), block]
-                remote(
-                    piece, piece, qsn.at[block // 2, e - 1], qrn.at[block // 2, e - 1], (f, speer(e))
-                ).wait_recv()
+        def _():
+            over_seq(across, block, 0, across).wait_recv()
+            over_seq(along, block, 1, along).wait_recv()
+            relay(block).start()
+
+    def take(k, right):
+        block, there, _, _ = chain(k, right)
+
+        @pl.when(there)
+        def _():
+            over_seq(corner, block, 2, along).wait_recv()
             over_core(block).start()
             total[...] += part(block)
 
+    other = f + 1 - 2 * c
+    total[...] = part(f)
+    for i, way in enumerate(ways):
+        stack_heads(i)
+        pass_on(*way)
+        if i == 1:
+            over_core(other).wait_recv()
+            total[...] += part(other)
+        if i > 0:
+            take(*ways[i - 1])
+    take(*ways[-1])
     for k, right in ways:
         block, there, _, _ = chain(k, right)
 
@@ -420,6 +443,10 @@
         def _(block=block):
             over_core(block + 1 - 2 * c).wait_recv()
             total[...] += part(block + 1 - 2 * c)
+
+    def halo_copy(g):
+        edge = kvbuf.at[g, pl.ds(WINDOW, WINDOW), :]
+        return remote(edge, kvbuf.at[g, pl.ds(0, WINDOW), :], hs.at[g], hr.at[g], (f, speer(1)))
 
     key_width = groups * HEAD_SIZE
     keys = turn(total[:, :key_width], cosine, sine, False).astype(jnp.bfloat16)
@@ -427,11 +454,8 @@
     for g in range(groups):
         lo, hi = g * HEAD_SIZE, (g + 1) * HEAD_SIZE
         kvbuf[g, WINDOW:, :] = jnp.concatenate([keys[:, lo:hi], values[:, lo:hi]], axis=1)
-    halo = remote(
-        kvbuf.at[:, pl.ds(WINDOW, WINDOW), :], kvbuf.at[:, pl.ds(0, WINDOW), :], hs, hr, (f, speer(1))
-    )
-    halo.start()
-    halo.wait()
+        halo_copy(g).start()
+    halo_copy(0).wait_recv()
     for e in range(1, ns):
         send(tokpad.at[speer(e)], tokblk.at[s], ts.at[e - 1], tr.at[e - 1], (f, speer(e)))
     before = speer(ns - 1)
@@ -441,6 +465,10 @@
         return remote(hg_out.at[g], hg_in.at[g], gsn.at[g], grn.at[g], (f, before))
 
     def attention(g):
+        @pl.when(g > 0)
+        def _():
+            halo_copy(g).wait_recv()
+
         kv = kvbuf[g]
         key, value = kv[:, :HEAD_SIZE], kv[:, HEAD_SIZE:]
         kv_t = kv.T
@@ -575,6 +603,7 @@
         cp.wait_send()
     for g in range(groups):
         hg_copy(g).wait_send()
+        halo_copy(g).wait_send()
         core_copy(g).wait_send()
         for e in range(1, ns):
             dkv_copy(g, e).wait_send()
@@ -593,8 +622,9 @@
                 @pl.when(there)
                 def _(k=k, right=right):
                     block = chain(k, right)[0]
-                    for e in range(1, ns):
-                        over_seq(block, e).wait_send()
+                    over_seq(s, block, 0, across).wait_send()
+                    over_seq(s, block, 1, along).wait_send()
+                    relay(block).wait_send()
                     over_core(block).wait_send()
 
     over_core(f).wait_send()
@@ -671,7 +701,7 @@
             sem((nz, ns - 1)), sem((nz, ns - 1)),
             sem((nz,)), sem((nz,)),
             sem((ns - 1,)), sem((ns - 1,)),
-            sem, sem,
+            sem((groups,)), sem((groups,)),
             sem((groups,)), sem((groups,)),
             sem((groups, ns - 1)), sem((groups, ns - 1)),
             sem((groups,)), sem((groups,)),

time: 67.9 us -> 73.2 us (1.078)
  Pallas kernels: 66.5 us -> 71.7 us
    pallas_call x1, Pallas kernels: 63.7 us -> 69 us  [fused(): pl.pallas_call(functools.partial(fused_kernel, nz, ns, share, pad), out_s...]
where the time goes in v1:
time: 73.2 us; the launch traced here: 73 us
  Pallas kernels  71.7 us (98%)
  between operations  1.29 us (2%)
    pallas_call x1, Pallas kernels, fused(): pl.pallas_call(functools.partial(fused_kernel, nz, ns, share, pad), out_s...  69 us
    pallas_call x1, Pallas kernels, fused(): pl.pallas_call(write_out, out_shape=tuple((shape(x.shape, x.dtype) for x...  2.76 us

profile of v1, /device:TPU:0, one launch (start us, length us, event | category | flops | bytes accessed | tf_op | source)
XLA Modules:
  0.0 73.0 jit_solution(12747126377006355478)
XLA Ops:
  1.3 69.0 %shard_map.93 = (bf16[128,2048]{1,0:T(8,128)(2,1)}, bf16[128,2048]{1,0:T(8,128)(2,1)}, bf16[2880,128]{1,0:T(8,128)(2,1)}, f32[360,128]{1,0:T(8,128)}) custom-call(bf16[2880,128]{1,0:T(8,128)(2,1)} %bitcast.11, bf16[128,2048]{1,0:T(8,128)(2,1)} %bitcast.12, bf16[360,512]{1,0:T(8,128)(2,1)} %w.1, f32[32]{0:T(128)} %sinks.1, s32[1]{0:T(128)S(6)} %copy.10.rolls, ...), custom_call_target="tpu_custom_call" | custom-call | tf_op jit(solution)/shard_map/pallas_call | solution.py:664
  70.3 2.8 %shard_map.94 = (bf16[128,2048]{1,0:T(8,128)(2,1)}, bf16[128,2048]{1,0:T(8,128)(2,1)}, bf16[2880,128]{1,0:T(8,128)(2,1)}, f32[360,128]{1,0:T(8,128)}) custom-call(bf16[128,2048]{1,0:T(8,128)(2,1)} %get-tuple-element.12.refs_0_, bf16[128,2048]{1,0:T(8,128)(2,1)} %get-tuple-element.13.refs_1_, bf16[2880,128]{1,0:T(8,128)(2,1)} %get-tuple-element.14.refs_2_, ...), custom_call_target="tpu_custom_call" | custom-call | tf_op jit(solution)/shard_map/pallas_call | solution.py:714

commit v2 on v0

--- a/solution.py
+++ b/solution.py
@@ -218,11 +218,29 @@
     return lax.dot_general(a, b, (((1,), (0,)), ((), ())), preferred_element_type=jnp.float32)
 
 
+def cos_sin(angle):
+    count = jnp.floor(angle * (2.0 / math.pi) + 0.5)
+    rest = angle - count * 1.5703125
+    rest = rest - count * 4.837512969970703125e-4
+    rest = rest - count * 7.54978995489188216e-8
+    z = rest * rest
+    s = rest + rest * z * ((-1.9515295891e-4 * z + 8.3321608736e-3) * z - 1.6666654611e-1)
+    c = 1.0 - 0.5 * z + z * z * ((2.443315711809948e-5 * z - 1.388731625493765e-3) * z + 4.166664568298827e-2)
+    quarter = count.astype(jnp.int32) & 3
+    odd = (quarter & 1) == 1
+    cosine = jnp.where(odd, s, c)
+    sine = jnp.where(odd, c, s)
+    return (
+        jnp.where((quarter == 1) | (quarter == 2), -cosine, cosine),
+        jnp.where(quarter >= 2, -sine, sine),
+    )
+
+
 def turn(x, cosine, sine, back):
     width = x.shape[1]
     lane = lax.broadcasted_iota(jnp.int32, x.shape, 1)
     swapped = jnp.where(
-        lane % HEAD_SIZE < HEAD_SIZE // 2,
+        (lane & (HEAD_SIZE - 1)) < HEAD_SIZE // 2,
         pltpu.roll(x, width - HEAD_SIZE // 2, 1),
         pltpu.roll(x, HEAD_SIZE // 2, 1),
     )
@@ -238,7 +256,7 @@
     nz, ns, share, pad,
     tok_hbm, q_hbm, w, sinks, rolls, og_hbm,
     attn_v, qgrad_v, tgrad_v, wgrad,
-    wall, tok, q, og, tokf, tokpad, tokblk, qs, gs, kvbuf, prob_t, dscore_t,
+    wall, tok, q, og, tokf, tokpad, tokblk, qs, qpair, gpair, kvbuf, prob_t, dscore_t,
     own_g, hg_out, hg_in, dkv_all, core_out, core_in, mine, zsum, z_out, z_in, total, esink,
     ins, rs_l, rr_l, rs_r, rr_r, qsn, qrn, ps, pr, ts, tr, hs, hr, gsn, grn, dsn, drn, cs, cr, rs, rr,
 ):
@@ -361,8 +379,7 @@
         s * rows + rolls[0] + lax.broadcasted_iota(jnp.int32, (rows, 128), 0), rows * ns
     )
     angle = position.astype(jnp.float32) * frequency
-    cosine = jnp.cos(angle)
-    sine = jnp.sin(angle)
+    cosine, sine = cos_sin(angle)
     sine = jnp.where(lane % HEAD_SIZE < HEAD_SIZE // 2, -sine, sine)
     for p in range(QUERY_HEADS // 2):
         pair = [jnp.full((1, rows), sinks[2 * p + i], jnp.float32) for i in range(2)]
@@ -384,11 +401,7 @@
     def _(g):
         here = lanes_of(g, span)
         x = turn(q[:, here].astype(jnp.float32), cosine, sine, False).astype(jnp.bfloat16)
-        x = x * jnp.asarray(HEAD_SIZE ** (-0.5), jnp.bfloat16)
-        o = og[:, here]
-        for h in range(per):
-            qs[g, h * rows : (h + 1) * rows, :] = x[:, h * HEAD_SIZE : (h + 1) * HEAD_SIZE]
-            gs[g, h * rows : (h + 1) * rows, :] = o[:, h * HEAD_SIZE : (h + 1) * HEAD_SIZE]
+        qs[:, here] = x * jnp.asarray(HEAD_SIZE ** (-0.5), jnp.bfloat16)
 
     def whole(block):
         return jnp.concatenate([wall[j, block] for j in range(ns)], axis=1)
@@ -445,10 +458,23 @@
         key, value = kv[:, :HEAD_SIZE], kv[:, HEAD_SIZE:]
         kv_t = kv.T
         key_t, value_t = kv_t[:HEAD_SIZE], kv_t[HEAD_SIZE:]
+        low = lax.broadcasted_iota(jnp.int32, kv.shape, 1) < HEAD_SIZE
+        none = jnp.zeros_like(kv)
+        swap = jnp.concatenate([value, key], axis=1)
+        keys2 = jnp.concatenate([jnp.where(low, kv, none), jnp.where(low, none, swap)], axis=0)
+        values2 = jnp.concatenate([jnp.where(low, swap, none), jnp.where(low, none, kv)], axis=0)
         slot = lax.broadcasted_iota(jnp.int32, (rows, 2 * rows), 0)
         at = lax.broadcasted_iota(jnp.int32, (rows, 2 * rows), 1) & (rows - 1)
         is_own = slot <= at
         valid = slot <= at + s * rows
+        first = low[:rows]
+        empty = none[:rows]
+
+        def side_by_side(x):
+            return jnp.concatenate([x[: rows + WINDOW], x[rows + WINDOW :]], axis=1)
+
+        def apart(x):
+            return jnp.concatenate([jnp.where(first, x, empty), jnp.where(first, empty, x)], axis=0)
 
         def chosen(x):
             return jnp.where(is_own, x[WINDOW:], x[:WINDOW])
@@ -459,11 +485,14 @@
 
         for p in range(per // 2):
             two = slice(p * 2 * rows, (p + 1) * 2 * rows)
-            query, grad = qs[g, two, :], gs[g, two, :]
-            expo = jnp.where(valid, jnp.exp(chosen(nt(key, query))), 0.0)
+            here = pl.ds(pl.multiple_of(g * span + p * 128, 128), 128)
+            query, grad = qs[:, here], og[:, here]
+            qpair[two, :] = apart(query)
+            gpair[two, :] = apart(grad)
+            expo = jnp.where(valid, jnp.exp(chosen(side_by_side(nt(keys2, query)))), 0.0)
             denominator = esink[g * (per // 2) + p] + jnp.sum(expo, axis=0, keepdims=True)
             probs = expo * (1.0 / denominator)
-            dprob = chosen(nt(value, grad))
+            dprob = chosen(side_by_side(nt(values2, grad)))
             delta = jnp.sum(probs * dprob, axis=0, keepdims=True)
             probs_b = spread(probs)
             dscore = spread(probs * (dprob - delta))
@@ -476,7 +505,11 @@
             here = pl.ds(pl.multiple_of(g * span + p * 128, 128), 128)
             attn_v[:, here] = out.astype(jnp.bfloat16)
             qgrad_v[:, here] = turn(dq, cosine, sine, True).astype(jnp.bfloat16)
-        dkv = jnp.concatenate([nn(dscore_t[...], qs[g]), nn(prob_t[...], gs[g])], axis=1)
+        dk = nn(dscore_t[...], qpair[...])
+        dv = nn(prob_t[...], gpair[...])
+        dkv = jnp.concatenate(
+            [dk[:, :HEAD_SIZE] + dk[:, HEAD_SIZE:], dv[:, :HEAD_SIZE] + dv[:, HEAD_SIZE:]], axis=1
+        )
         hg_out[g] = dkv[:WINDOW].astype(jnp.bfloat16)
         own_g[g] = dkv[WINDOW:]
         hg_copy(g).start()
@@ -649,8 +682,9 @@
             vm((nf, rows, -(-krows // 128) * 128), bf),
             vm((ns, nf * pad, rows), bf),
             vm((ns, nf * pad, rows), bf),
-            vm((groups, per * rows, HEAD_SIZE), bf),
-            vm((groups, per * rows, HEAD_SIZE), bf),
+            vm((rows, query_width), bf),
+            vm((per * rows, 2 * HEAD_SIZE), bf),
+            vm((per * rows, 2 * HEAD_SIZE), bf),
             vm((groups, rows + WINDOW, 2 * HEAD_SIZE), bf),
             vm((rows + WINDOW, per * rows), bf),
             vm((rows + WINDOW, per * rows), bf),

time: 67.9 us -> 68 us (level)
  no operation moved by 1% of the time
where the time goes in v2:
time: 68 us; the launch traced here: 67.9 us
  Pallas kernels  66.6 us (98%)
  between operations  1.29 us (2%)
    pallas_call x1, Pallas kernels, fused(): pl.pallas_call(functools.partial(fused_kernel, nz, ns, share, pad), out_s...  63.8 us
    pallas_call x1, Pallas kernels, fused(): pl.pallas_call(write_out, out_shape=tuple((shape(x.shape, x.dtype) for x...  2.76 us

profile of v2, /device:TPU:0, one launch (start us, length us, event | category | flops | bytes accessed | tf_op | source)
XLA Modules:
  0.0 67.9 jit_solution(15899636500023593741)
XLA Ops:
  1.3 63.8 %shard_map.93 = (bf16[128,2048]{1,0:T(8,128)(2,1)}, bf16[128,2048]{1,0:T(8,128)(2,1)}, bf16[2880,128]{1,0:T(8,128)(2,1)}, f32[360,128]{1,0:T(8,128)}) custom-call(bf16[2880,128]{1,0:T(8,128)(2,1)} %bitcast.11, bf16[128,2048]{1,0:T(8,128)(2,1)} %bitcast.12, bf16[360,512]{1,0:T(8,128)(2,1)} %w.1, f32[32]{0:T(128)} %sinks.1, s32[1]{0:T(128)S(6)} %copy.10.rolls, ...), custom_call_target="tpu_custom_call" | custom-call | tf_op jit(solution)/shard_map/pallas_call | solution.py:667
  65.1 2.8 %shard_map.94 = (bf16[128,2048]{1,0:T(8,128)(2,1)}, bf16[128,2048]{1,0:T(8,128)(2,1)}, bf16[2880,128]{1,0:T(8,128)(2,1)}, f32[360,128]{1,0:T(8,128)}) custom-call(bf16[128,2048]{1,0:T(8,128)(2,1)} %get-tuple-element.12.refs_0_, bf16[128,2048]{1,0:T(8,128)(2,1)} %get-tuple-element.13.refs_1_, bf16[2880,128]{1,0:T(8,128)(2,1)} %get-tuple-element.14.refs_2_, ...), custom_call_target="tpu_custom_call" | custom-call | tf_op jit(solution)/shard_map/pallas_call | solution.py:718
